TPU v7x, 32 devices: a whole 2x2x4 slice. The times are simulated.
32 devices in a mesh: groups: 2 (over y), blk: 8 (over z, x), sector: 2 (over core).
Axes of the slice: x: 2, y: 2, z: 4, core: 2. Of those that a mesh axis runs over, the one named last changes fastest.
Arguments:
- wavefunction: bfloat16 [4096, 768], P(('groups', 'blk')), parts along dimension 0
- env_left: bfloat16 [16, 8, 2, 256, 256], P(('groups', 'blk'), None, 'sector'), parts along dimension 0
- pattern: int32 [16, 8, 2], P(('groups', 'blk'), None, 'sector'), parts along dimension 0, may hold values 0 or 1
- env_right: bfloat16 [16, 2, 768, 768], P(('groups', 'blk'), 'sector'), parts along dimension 0
- energy: float32 [16], P(('groups', 'blk')), parts along dimension 0, may hold values from 0.5 to 2
- block_rows: int32 [16], P(('groups', 'blk')), parts along dimension 0, may hold values from 64 to 256, as said below
Outputs:
- residual: float32 [4096, 768], P(('groups', 'blk', 'sector')), parts along dimension 0
- rayleigh: float32 [2], P('groups'), parts along dimension 0
There are 2 independent parts, one for each index of `groups`. A program takes and returns all parts, laid end to end along the dimension named above; each array names one. Nothing has to cross between parts.
Inputs may be any that keep to these rules, and one draw needn't show every extreme that they name: `block_rows`: rows of a block at or past its entry are padding.
All inputs are finite; a program needn't handle non-finite values. No bound on the sum of `pattern` on one device may be relied on, other than what follows from the above.
Results may differ from a plain program's by a relative error of at most 0.0003.
Values may be sent and summed in bfloat16 or wider, within the bound.
A program may use at most 64 MiB of HBM per device.

v0:
```python
import jax
import jax.numpy as jnp
from jax import lax
from jax.sharding import PartitionSpec as P


def from_behind(value, axis, steps):
    count = lax.axis_size(axis)
    pairs = [(source, (source + steps) % count) for source in range(count)]
    return lax.ppermute(value, axis, pairs)


def shards(wavefunction, env_left, pattern, env_right, energy, block_rows):
    rows_pad = env_left.shape[-1]
    loop_len = env_left.shape[1]
    middle = loop_len // 2
    half_rows = rows_pad // 2
    live_rows = (jnp.arange(rows_pad) < block_rows[0]).astype(jnp.bfloat16)
    own_block = wavefunction * live_rows[:, None]
    coupled = env_left[0, :, 0] * pattern[0, :, 0].astype(jnp.bfloat16)[:, None, None]
    core_index = lax.axis_index("sector")
    own_half = lax.dynamic_slice_in_dim(own_block, core_index * half_rows, half_rows, 0)

    def add_term(summed_now, slot, pieces):
        term_env = lax.dynamic_index_in_dim(coupled, slot, 0, keepdims=False)
        return summed_now + jnp.dot(term_env, pieces, preferred_element_type=jnp.float32)

    moving = from_behind(own_block, "blk", middle)
    summed = jnp.zeros((rows_pad, own_block.shape[1]), jnp.float32)
    summed = add_term(summed, 0, moving)

    def advance(turn, state):
        moving_now, summed_now = state
        moving_now = from_behind(moving_now, "blk", -1)
        return (moving_now, add_term(summed_now, turn, moving_now))

    moving, summed = lax.fori_loop(1, loop_len, advance, (moving, summed))
    partial_sigma = jnp.dot(
        summed,
        env_right[0, 0].astype(jnp.float32),
        precision=lax.Precision.HIGHEST,
        preferred_element_type=jnp.float32,
    )
    summed_terms = lax.psum(partial_sigma, "sector")
    mine = lax.dynamic_slice_in_dim(summed_terms, core_index * half_rows, half_rows, 0)
    live_half = lax.dynamic_slice_in_dim(live_rows, core_index * half_rows, half_rows, 0).astype(
        jnp.float32
    )
    own_wide = own_half.astype(jnp.float32)
    sigma_half = (mine + energy[0] * own_wide) * live_half[:, None]
    correlation, norm_sq = lax.psum(
        (jnp.sum(own_wide * sigma_half), jnp.sum(own_wide * own_wide)), ("blk", "sector")
    )
    rayleigh = correlation / norm_sq
    residual = sigma_half - rayleigh * own_wide
    return (residual, rayleigh.reshape(1))


def solution(mesh):
    return jax.shard_map(
        shards,
        mesh=mesh,
        in_specs=(
            P(("groups", "blk"), None),
            P(("groups", "blk"), None, "sector", None, None),
            P(("groups", "blk"), None, "sector"),
            P(("groups", "blk"), "sector", None, None),
            P(("groups", "blk")),
            P(("groups", "blk")),
        ),
        out_specs=(P(("groups", "blk", "sector"), None), P("groups")),
        check_vma=False,
    )
```

profile of v0, /device:TPU:0, one launch (start us, length us, event | category | flops | bytes accessed | tf_op | source)
XLA Modules:
  0.0 192.4 jit_solution(15781417668310196435)
XLA Ops:
  8.0 1.1 broadcast_multiply_fusion
  9.1 4.1 %collective-permute-start.1 = (bf16[256,768]{1,0:T(8,128)(2,1)S(1)}, bf16[256,768]{1,0:T(8,128)(2,1)}, u32[]{:S(2)}, u32[]{:S(2)}) collective-permute-start(bf16[256,768]{1,0:T(8,128)(2,1)S(1)} %broadcast_multiply_fusion), channel_id=1, source_target_pairs={{0,8},{2,10},{4,12},{6,14},{8,0},{10,2},{12,4},{14,6},{1,9},{3,11}... | collective-permute-start | bytes 1179656 | tf_op jit(solution)/shard_map/ppermute | solution.py:10
  13.8 1.4 bitcast_multiply_fusion
  15.2 15.6 %collective-permute-done.1 = bf16[256,768]{1,0:T(8,128)(2,1)} collective-permute-done((bf16[256,768]{1,0:T(8,128)(2,1)S(1)}, bf16[256,768]{1,0:T(8,128)(2,1)}, u32[]{:S(2)}, u32[]{:S(2)}) %collective-permute-start.1) | collective-permute-done | bytes 393248 | tf_op jit(solution)/shard_map/ppermute | solution.py:10
  30.8 1.3 fusion.10
  32.1 89.6 %while.17 = (s32[]{:T(128)}, bf16[256,768]{1,0:T(8,128)(2,1)}, f32[256,768]{1,0:T(8,128)S(1)}, bf16[8,256,256]{2,1,0:T(8,128)(2,1)S(1)}, s32[]{:T(128)}, /*index=5*/s32[]{:T(128)}, s32[]{:T(128)}) while((s32[]{:T(128)}, bf16[256,768]{1,0:T(8,128)(2,1)}, f32[256,768]{1,0:T(8,128)S(1)}, bf16[8,256,256]{2,1,0:T(8,128)(2,1)S(1)}, s32[]{:T(128)}, ...), condition=%wide.region_1.2_spmd, body=%wide.region_0.1_spmd.sunk | while | flops 100859904 | bytes 4456611 | solution.py:37
  32.1 4.5 %collective-permute-start = (bf16[256,768]{1,0:T(8,128)(2,1)}, bf16[256,768]{1,0:T(8,128)(2,1)S(1)}, u32[]{:S(2)}, u32[]{:S(2)}) collective-permute-start(bf16[256,768]{1,0:T(8,128)(2,1)} %get-tuple-element.158), channel_id=1, source_target_pairs={{0,14},{2,0},{4,2},{6,4},{8,6},{10,8},{12,10},{14,12},{1,15},{3,1}... | collective-permute-start | bytes 1179656 | tf_op jit(solution)/shard_map/while/body/eval_jaxpr/ppermute | solution.py:10
  36.6 8.9 %collective-permute-done = bf16[256,768]{1,0:T(8,128)(2,1)S(1)} collective-permute-done((bf16[256,768]{1,0:T(8,128)(2,1)}, bf16[256,768]{1,0:T(8,128)(2,1)S(1)}, u32[]{:S(2)}, u32[]{:S(2)}) %collective-permute-start) | collective-permute-done | bytes 393248 | tf_op jit(solution)/shard_map/while/body/eval_jaxpr/ppermute | solution.py:10
  45.5 0.7 copy.15
  46.5 5.1 %collective-permute-start = (bf16[256,768]{1,0:T(8,128)(2,1)}, bf16[256,768]{1,0:T(8,128)(2,1)S(1)}, u32[]{:S(2)}, u32[]{:S(2)}) collective-permute-start(bf16[256,768]{1,0:T(8,128)(2,1)} %get-tuple-element.158), channel_id=1, source_target_pairs={{0,14},{2,0},{4,2},{6,4},{8,6},{10,8},{12,10},{14,12},{1,15},{3,1}... | collective-permute-start | bytes 1179656 | tf_op jit(solution)/shard_map/while/body/eval_jaxpr/ppermute | solution.py:10
  51.7 8.0 %collective-permute-done = bf16[256,768]{1,0:T(8,128)(2,1)S(1)} collective-permute-done((bf16[256,768]{1,0:T(8,128)(2,1)}, bf16[256,768]{1,0:T(8,128)(2,1)S(1)}, u32[]{:S(2)}, u32[]{:S(2)}) %collective-permute-start) | collective-permute-done | bytes 393248 | tf_op jit(solution)/shard_map/while/body/eval_jaxpr/ppermute | solution.py:10
  59.7 0.7 copy.15
  60.7 5.1 %collective-permute-start = (bf16[256,768]{1,0:T(8,128)(2,1)}, bf16[256,768]{1,0:T(8,128)(2,1)S(1)}, u32[]{:S(2)}, u32[]{:S(2)}) collective-permute-start(bf16[256,768]{1,0:T(8,128)(2,1)} %get-tuple-element.158), channel_id=1, source_target_pairs={{0,14},{2,0},{4,2},{6,4},{8,6},{10,8},{12,10},{14,12},{1,15},{3,1}... | collective-permute-start | bytes 1179656 | tf_op jit(solution)/shard_map/while/body/eval_jaxpr/ppermute | solution.py:10
  65.9 7.1 %collective-permute-done = bf16[256,768]{1,0:T(8,128)(2,1)S(1)} collective-permute-done((bf16[256,768]{1,0:T(8,128)(2,1)}, bf16[256,768]{1,0:T(8,128)(2,1)S(1)}, u32[]{:S(2)}, u32[]{:S(2)}) %collective-permute-start) | collective-permute-done | bytes 393248 | tf_op jit(solution)/shard_map/while/body/eval_jaxpr/ppermute | solution.py:10
  73.0 0.7 copy.15
  74.0 5.1 %collective-permute-start = (bf16[256,768]{1,0:T(8,128)(2,1)}, bf16[256,768]{1,0:T(8,128)(2,1)S(1)}, u32[]{:S(2)}, u32[]{:S(2)}) collective-permute-start(bf16[256,768]{1,0:T(8,128)(2,1)} %get-tuple-element.158), channel_id=1, source_target_pairs={{0,14},{2,0},{4,2},{6,4},{8,6},{10,8},{12,10},{14,12},{1,15},{3,1}... | collective-permute-start | bytes 1179656 | tf_op jit(solution)/shard_map/while/body/eval_jaxpr/ppermute | solution.py:10
  79.1 6.2 %collective-permute-done = bf16[256,768]{1,0:T(8,128)(2,1)S(1)} collective-permute-done((bf16[256,768]{1,0:T(8,128)(2,1)}, bf16[256,768]{1,0:T(8,128)(2,1)S(1)}, u32[]{:S(2)}, u32[]{:S(2)}) %collective-permute-start) | collective-permute-done | bytes 393248 | tf_op jit(solution)/shard_map/while/body/eval_jaxpr/ppermute | solution.py:10
  85.3 0.7 copy.15
  86.4 5.1 %collective-permute-start = (bf16[256,768]{1,0:T(8,128)(2,1)}, bf16[256,768]{1,0:T(8,128)(2,1)S(1)}, u32[]{:S(2)}, u32[]{:S(2)}) collective-permute-start(bf16[256,768]{1,0:T(8,128)(2,1)} %get-tuple-element.158), channel_id=1, source_target_pairs={{0,14},{2,0},{4,2},{6,4},{8,6},{10,8},{12,10},{14,12},{1,15},{3,1}... | collective-permute-start | bytes 1179656 | tf_op jit(solution)/shard_map/while/body/eval_jaxpr/ppermute | solution.py:10
  91.5 5.6 %collective-permute-done = bf16[256,768]{1,0:T(8,128)(2,1)S(1)} collective-permute-done((bf16[256,768]{1,0:T(8,128)(2,1)}, bf16[256,768]{1,0:T(8,128)(2,1)S(1)}, u32[]{:S(2)}, u32[]{:S(2)}) %collective-permute-start) | collective-permute-done | bytes 393248 | tf_op jit(solution)/shard_map/while/body/eval_jaxpr/ppermute | solution.py:10
  97.1 0.7 copy.15
  98.1 5.1 %collective-permute-start = (bf16[256,768]{1,0:T(8,128)(2,1)}, bf16[256,768]{1,0:T(8,128)(2,1)S(1)}, u32[]{:S(2)}, u32[]{:S(2)}) collective-permute-start(bf16[256,768]{1,0:T(8,128)(2,1)} %get-tuple-element.158), channel_id=1, source_target_pairs={{0,14},{2,0},{4,2},{6,4},{8,6},{10,8},{12,10},{14,12},{1,15},{3,1}... | collective-permute-start | bytes 1179656 | tf_op jit(solution)/shard_map/while/body/eval_jaxpr/ppermute | solution.py:10
  103.3 5.6 %collective-permute-done = bf16[256,768]{1,0:T(8,128)(2,1)S(1)} collective-permute-done((bf16[256,768]{1,0:T(8,128)(2,1)}, bf16[256,768]{1,0:T(8,128)(2,1)S(1)}, u32[]{:S(2)}, u32[]{:S(2)}) %collective-permute-start) | collective-permute-done | bytes 393248 | tf_op jit(solution)/shard_map/while/body/eval_jaxpr/ppermute | solution.py:10
  108.9 0.7 copy.15
  109.9 5.1 %collective-permute-start = (bf16[256,768]{1,0:T(8,128)(2,1)}, bf16[256,768]{1,0:T(8,128)(2,1)S(1)}, u32[]{:S(2)}, u32[]{:S(2)}) collective-permute-start(bf16[256,768]{1,0:T(8,128)(2,1)} %get-tuple-element.158), channel_id=1, source_target_pairs={{0,14},{2,0},{4,2},{6,4},{8,6},{10,8},{12,10},{14,12},{1,15},{3,1}... | collective-permute-start | bytes 1179656 | tf_op jit(solution)/shard_map/while/body/eval_jaxpr/ppermute | solution.py:10
  115.0 5.6 %collective-permute-done = bf16[256,768]{1,0:T(8,128)(2,1)S(1)} collective-permute-done((bf16[256,768]{1,0:T(8,128)(2,1)}, bf16[256,768]{1,0:T(8,128)(2,1)S(1)}, u32[]{:S(2)}, u32[]{:S(2)}) %collective-permute-start) | collective-permute-done | bytes 393248 | tf_op jit(solution)/shard_map/while/body/eval_jaxpr/ppermute | solution.py:10
  120.6 0.7 copy.15
  121.7 2.0 %fusion.3 = f32[256,768]{1,0:T(8,128)} fusion(f32[256,768]{1,0:T(8,128)S(1)} %get-tuple-element.112, bf16[1,1,768,768]{3,2,1,0:T(8,128)(2,1)S(1)} %copy-done), kind=kOutput, calls=%fused_computation.4 | convolution fusion | flops 1811939328 | bytes 2752512 | tf_op jit(solution)/shard_map/dot_general | solution.py:38
  124.5 20.4 %all-reduce.3.cloned.1.call-done = f32[256,768]{1,0:T(8,128)} async-done(((f32[256,768]{1,0:T(8,128)}), f32[256,768]{1,0:T(8,128)}) %all-reduce.3.cloned.1.call-update) | async-done | bytes 786448 | tf_op jit(solution)/shard_map/psum | solution.py:44
  144.9 1.8 fusion.8
  146.7 34.5 %all-reduce = (f32[]{:T(128)}, f32[]{:T(128)}) all-reduce(f32[]{:T(128)} %get-tuple-element.114, f32[]{:T(128)} %get-tuple-element.113), channel_id=1, replica_groups=mesh['groups'=2,'blk'=8,'sector'=2] {'blk','sector'}, use_global_device_ids=true, to_apply=%region_4.5 | all-reduce | flops 2 | bytes 16 | tf_op jit(solution)/shard_map/psum | solution.py:51
  182.5 1.9 fusion.9
  (18 shorter events, 2.8 us)
Async XLA Ops:
  7.2 114.5 %copy-start = (bf16[1,1,768,768]{3,2,1,0:T(8,128)(2,1)S(1)}, bf16[1,1,768,768]{3,2,1,0:T(8,128)(2,1)}, u32[]{:S(2)}) copy-start(bf16[1,1,768,768]{3,2,1,0:T(8,128)(2,1)} %param.11) | copy-start | bytes 3538948
  7.2 137.7 %all-reduce.3.cloned.1.call-start = ((), (), s32[]{:S(2)}) async-start(), calls=%async_computation | async-start | bytes 1572864 | tf_op jit(solution)/shard_map/psum | solution.py:44
  9.1 23.0 %copy-start.1 = (bf16[256,768]{1,0:T(8,128)(2,1)}, bf16[256,768]{1,0:T(8,128)(2,1)S(1)}, u32[]{:S(2)}) copy-start(bf16[256,768]{1,0:T(8,128)(2,1)S(1)} %broadcast_multiply_fusion) | copy-start | bytes 1179652
  9.1 21.7 %collective-permute-start.1 = (bf16[256,768]{1,0:T(8,128)(2,1)S(1)}, bf16[256,768]{1,0:T(8,128)(2,1)}, u32[]{:S(2)}, u32[]{:S(2)}) collective-permute-start(bf16[256,768]{1,0:T(8,128)(2,1)S(1)} %broadcast_multiply_fusion), channel_id=1, source_target_pairs={{0,8},{2,10},{4,12},{6,14},{8,0},{10,2},{12,4},{14,6},{1,9},{3,11}... | collective-permute-start | bytes 1179656 | tf_op jit(solution)/shard_map/ppermute | solution.py:10
  32.1 13.4 %collective-permute-start = (bf16[256,768]{1,0:T(8,128)(2,1)}, bf16[256,768]{1,0:T(8,128)(2,1)S(1)}, u32[]{:S(2)}, u32[]{:S(2)}) collective-permute-start(bf16[256,768]{1,0:T(8,128)(2,1)} %get-tuple-element.158), channel_id=1, source_target_pairs={{0,14},{2,0},{4,2},{6,4},{8,6},{10,8},{12,10},{14,12},{1,15},{3,1}... | collective-permute-start | bytes 1179656 | tf_op jit(solution)/shard_map/while/body/eval_jaxpr/ppermute | solution.py:10
  46.5 13.2 %collective-permute-start = (bf16[256,768]{1,0:T(8,128)(2,1)}, bf16[256,768]{1,0:T(8,128)(2,1)S(1)}, u32[]{:S(2)}, u32[]{:S(2)}) collective-permute-start(bf16[256,768]{1,0:T(8,128)(2,1)} %get-tuple-element.158), channel_id=1, source_target_pairs={{0,14},{2,0},{4,2},{6,4},{8,6},{10,8},{12,10},{14,12},{1,15},{3,1}... | collective-permute-start | bytes 1179656 | tf_op jit(solution)/shard_map/while/body/eval_jaxpr/ppermute | solution.py:10
  60.7 12.2 %collective-permute-start = (bf16[256,768]{1,0:T(8,128)(2,1)}, bf16[256,768]{1,0:T(8,128)(2,1)S(1)}, u32[]{:S(2)}, u32[]{:S(2)}) collective-permute-start(bf16[256,768]{1,0:T(8,128)(2,1)} %get-tuple-element.158), channel_id=1, source_target_pairs={{0,14},{2,0},{4,2},{6,4},{8,6},{10,8},{12,10},{14,12},{1,15},{3,1}... | collective-permute-start | bytes 1179656 | tf_op jit(solution)/shard_map/while/body/eval_jaxpr/ppermute | solution.py:10
  74.0 11.3 %collective-permute-start = (bf16[256,768]{1,0:T(8,128)(2,1)}, bf16[256,768]{1,0:T(8,128)(2,1)S(1)}, u32[]{:S(2)}, u32[]{:S(2)}) collective-permute-start(bf16[256,768]{1,0:T(8,128)(2,1)} %get-tuple-element.158), channel_id=1, source_target_pairs={{0,14},{2,0},{4,2},{6,4},{8,6},{10,8},{12,10},{14,12},{1,15},{3,1}... | collective-permute-start | bytes 1179656 | tf_op jit(solution)/shard_map/while/body/eval_jaxpr/ppermute | solution.py:10
  86.4 10.7 %collective-permute-start = (bf16[256,768]{1,0:T(8,128)(2,1)}, bf16[256,768]{1,0:T(8,128)(2,1)S(1)}, u32[]{:S(2)}, u32[]{:S(2)}) collective-permute-start(bf16[256,768]{1,0:T(8,128)(2,1)} %get-tuple-element.158), channel_id=1, source_target_pairs={{0,14},{2,0},{4,2},{6,4},{8,6},{10,8},{12,10},{14,12},{1,15},{3,1}... | collective-permute-start | bytes 1179656 | tf_op jit(solution)/shard_map/while/body/eval_jaxpr/ppermute | solution.py:10
  98.1 10.7 %collective-permute-start = (bf16[256,768]{1,0:T(8,128)(2,1)}, bf16[256,768]{1,0:T(8,128)(2,1)S(1)}, u32[]{:S(2)}, u32[]{:S(2)}) collective-permute-start(bf16[256,768]{1,0:T(8,128)(2,1)} %get-tuple-element.158), channel_id=1, source_target_pairs={{0,14},{2,0},{4,2},{6,4},{8,6},{10,8},{12,10},{14,12},{1,15},{3,1}... | collective-permute-start | bytes 1179656 | tf_op jit(solution)/shard_map/while/body/eval_jaxpr/ppermute | solution.py:10
  109.9 10.7 %collective-permute-start = (bf16[256,768]{1,0:T(8,128)(2,1)}, bf16[256,768]{1,0:T(8,128)(2,1)S(1)}, u32[]{:S(2)}, u32[]{:S(2)}) collective-permute-start(bf16[256,768]{1,0:T(8,128)(2,1)} %get-tuple-element.158), channel_id=1, source_target_pairs={{0,14},{2,0},{4,2},{6,4},{8,6},{10,8},{12,10},{14,12},{1,15},{3,1}... | collective-permute-start | bytes 1179656 | tf_op jit(solution)/shard_map/while/body/eval_jaxpr/ppermute | solution.py:10
  121.7 23.2 %copy-start.2 = (bf16[256,768]{1,0:T(8,128)(2,1)S(1)}, bf16[256,768]{1,0:T(8,128)(2,1)}, u32[]{:S(2)}) copy-start(bf16[256,768]{1,0:T(8,128)(2,1)} %copy-done.1) | copy-start | bytes 1179652
Sparse Core Ops, SparseCore 0:
  123.9 21.0 all-reduce.2
where the time goes:
time: 193 us; the launch traced here: 192 us
  waiting for transfers between devices  83.1 us (43%)
  starting transfers between devices  39.4 us (20%)
  blocking collectives  34.5 us (18%)
  between operations  18 us (9%)
  other arithmetic  6.83 us (4%)
  matrix products  5.26 us (3%)
  local copies, waits for them, and re-layouts  5.18 us (3%)
    ppermute x8, waiting for transfers between devices, from_behind(): return lax.ppermute(value, axis, pairs)  62.6 us
    ppermute x8, starting transfers between devices, from_behind(): return lax.ppermute(value, axis, pairs)  39.4 us
    psum x1, blocking collectives, shards(): lax.psum((jnp.sum(own_wide * sigma_half), jnp.sum(own_wide * own_wide)),...  34.5 us
    psum x1, waiting for transfers between devices, shards(): summed_terms = lax.psum(partial_sigma, 'sector')  20.4 us
    while x7, local copies, waits for them, and re-layouts  5.16 us
  transfers between devices with their start and end apart: 9, of which 9 were waited for; matrix products, arithmetic and copies ran while one was open for 1% of the time, Pallas kernels for 0%

commit v1 on v0

--- a/solution.py
+++ b/solution.py
@@ -1,7 +1,13 @@
+import functools
+
 import jax
 import jax.numpy as jnp
 from jax import lax
+from jax.experimental import pallas as pl
+from jax.experimental.pallas import tpu as pltpu
 from jax.sharding import PartitionSpec as P
+
+DOWN, UP, ACROSS = 0, 1, 2
 
 
 def from_behind(value, axis, steps):
@@ -10,7 +16,7 @@
     return lax.ppermute(value, axis, pairs)
 
 
-def shards(wavefunction, env_left, pattern, env_right, energy, block_rows):
+def ring_shards(wavefunction, env_left, pattern, env_right, energy, block_rows):
     rows_pad = env_left.shape[-1]
     loop_len = env_left.shape[1]
     middle = loop_len // 2
@@ -56,7 +62,327 @@
     return (residual, rayleigh.reshape(1))
 
 
+def row_pieces(rows):
+    across = rows * 3 // 16 // 16 * 16
+    line = rows - across
+    front = (line // 2 + 15) // 16 * 16
+    return [(0, front), (front, line - front)], [(line, across)]
+
+
+def kernel(
+    n,
+    wave_hbm,
+    left_hbm,
+    right_hbm,
+    pattern,
+    energy,
+    block_rows,
+    residual,
+    rayleigh,
+    wave,
+    blocks,
+    left,
+    right,
+    acc,
+    part_out,
+    part_in,
+    part_own,
+    stats,
+    local_sem,
+    send_sem,
+    recv_sem,
+    pair_send,
+    pair_recv,
+    stat_send,
+    stat_recv,
+):
+    lines = n // 2
+    rows, cols = wave.shape
+    half_rows, half_cols = rows // 2, cols // 2
+    middle = n // 2
+    core = lax.axis_index("sector")
+    me = lax.axis_index("blk")
+    other = 1 - core
+    z, x = me // 2, me % 2
+    beside = me + 1 - 2 * x
+    rank = me * 2 + core
+    line_first, across_first = row_pieces(rows)
+    pieces = line_first + across_first
+    n_line = len(line_first)
+    has = {DOWN: z > 0, UP: z < lines - 1, ACROSS: None}
+    toward = {DOWN: me - 2, UP: me + 2, ACROSS: beside}
+
+    wave_copy = pltpu.make_async_copy(wave_hbm, wave, local_sem.at[0])
+    left_copy = pltpu.make_async_copy(
+        left_hbm.at[0, :, 0], left.at[:, pl.ds(core * rows, rows)], local_sem.at[1]
+    )
+    right_copy = pltpu.make_async_copy(
+        right_hbm.at[0, 0, pl.ds(core * half_cols, half_cols)], right.at[core], local_sem.at[2]
+    )
+    wave_copy.start()
+    left_copy.start()
+    right_copy.start()
+
+    barrier = pltpu.get_barrier_semaphore()
+    for step in range(1, 2 * n):
+        peer = lax.rem(rank + step, 2 * n)
+        pl.semaphore_signal(
+            barrier,
+            inc=1,
+            device_id={"blk": peer // 2, "sector": peer % 2},
+            device_id_type=pl.DeviceIdType.MESH,
+        )
+
+    wave_copy.wait()
+    row_ids = lax.broadcasted_iota(jnp.int32, (rows, cols), 0)
+    wave[...] = jnp.where(row_ids < block_rows[0], wave[...].astype(jnp.float32), 0.0).astype(
+        wave.dtype
+    )
+    blocks[me] = wave[:, pl.ds(pl.multiple_of(core * half_cols, half_cols), half_cols)]
+    pl.semaphore_wait(barrier, 2 * n - 1)
+
+    sent = []
+
+    def under(condition, action):
+        if condition is None:
+            action()
+        else:
+            pl.when(condition)(action)
+
+    def both(first, second):
+        if first is None:
+            return second
+        if second is None:
+            return first
+        return jnp.logical_and(first, second)
+
+    def block_copy(block, piece, way):
+        start, size = pieces[piece]
+        part = blocks.at[block, pl.ds(start, size)]
+        return pltpu.make_async_remote_copy(
+            src_ref=part,
+            dst_ref=part,
+            send_sem=send_sem.at[block, piece, way],
+            recv_sem=recv_sem.at[block, piece],
+            device_id={"blk": toward[way], "sector": core},
+            device_id_type=pl.DeviceIdType.MESH,
+        )
+
+    def send(block, piece, way, condition=None):
+        condition = both(condition, has[way])
+        under(condition, lambda: block_copy(block, piece, way).start())
+        sent.append((block, piece, way, condition))
+
+    def receive(block, piece, condition=None):
+        under(condition, lambda: block_copy(block, piece, ACROSS).wait_recv())
+
+    for piece in range(n_line):
+        for way in (DOWN, UP, ACROSS):
+            send(me, piece, way)
+    for piece in range(n_line, len(pieces)):
+        for way in (ACROSS, DOWN, UP):
+            send(me, piece, way)
+
+    def pair_copy(source, target, index):
+        return pltpu.make_async_remote_copy(
+            src_ref=source,
+            dst_ref=target,
+            send_sem=pair_send.at[index],
+            recv_sem=pair_recv.at[index],
+            device_id={"sector": other},
+            device_id_type=pl.DeviceIdType.MESH,
+        )
+
+    left_copy.wait()
+    for slot in range(n):
+        mine = left[slot, pl.ds(core * rows, rows)].astype(jnp.float32)
+        left[slot, pl.ds(core * rows, rows)] = (
+            mine * pattern[0, slot, 0].astype(jnp.float32)
+        ).astype(left.dtype)
+    own_left = left.at[:, pl.ds(core * rows, rows)]
+    left_out = pair_copy(own_left, own_left, 0)
+    left_out.start()
+    right_out = pair_copy(
+        right_hbm.at[0, 0, pl.ds(other * half_cols, half_cols)], right.at[core], 1
+    )
+    right_out.start()
+
+    def accumulate(block, condition=None, fresh=False):
+        def action():
+            slot = lax.rem(block - me + middle + n, n)
+            product = jnp.dot(left[slot], blocks[block], preferred_element_type=jnp.float32)
+            acc[...] = product if fresh else acc[...] + product
+
+        under(condition, action)
+
+    def forward(distance):
+        sides = (
+            (me + 2 * distance, z + distance < lines, DOWN),
+            (me - 2 * distance, z >= distance, UP),
+        )
+        for piece in range(n_line):
+            for block, condition, way in sides:
+                receive(block, piece, condition)
+                send(block, piece, way, condition)
+                send(block, piece, ACROSS, condition)
+        for piece in range(n_line, len(pieces)):
+            if distance == 1:
+                receive(beside, piece)
+                send(beside, piece, DOWN)
+                send(beside, piece, UP)
+            for block, condition, way in sides:
+                for source in (block, block + 1 - 2 * x):
+                    receive(source, piece, condition)
+                    send(source, piece, way, condition)
+
+    def compute(distance):
+        if distance < lines:
+            accumulate(me + 2 * distance, z + distance < lines)
+            accumulate(me - 2 * distance, z >= distance)
+        near = distance - 1
+        sides = [(beside, None)]
+        if near:
+            sides = [(beside + 2 * near, z + near < lines), (beside - 2 * near, z >= near)]
+        for block, condition in sides:
+            for piece in range(n_line):
+                receive(block, piece, condition)
+            accumulate(block, condition)
+
+    forward(1)
+    left_out.wait_recv()
+    accumulate(me, fresh=True)
+    for distance in range(2, lines):
+        forward(distance)
+        compute(distance - 1)
+    compute(lines - 1)
+    compute(lines)
+
+    right_copy.wait()
+    right_out.wait_recv()
+
+    def finish(first):
+        total = None
+        for term in range(2):
+            wide = acc[pl.ds(pl.multiple_of(term * rows + first, half_rows), half_rows)]
+            high = wide.astype(jnp.bfloat16)
+            low = (wide - high.astype(jnp.float32)).astype(jnp.bfloat16)
+            both_parts = jnp.concatenate([high, low], axis=0)
+            product = jnp.dot(both_parts, right[term], preferred_element_type=jnp.float32)
+            product = product[:half_rows] + product[half_rows:]
+            total = product if total is None else total + product
+        return total
+
+    def lanes(values):
+        summed = values[:, 0:128]
+        for column in range(128, cols, 128):
+            summed = summed + values[:, column : column + 128]
+        return jnp.sum(summed, axis=0, keepdims=True)
+
+    first_other = pl.multiple_of(other * half_rows, half_rows)
+    first_own = pl.multiple_of(core * half_rows, half_rows)
+    partial_other = finish(first_other)
+    part_out[...] = partial_other
+    part_copy = pair_copy(part_out, part_in, 2)
+    part_copy.start()
+    partial_own = finish(first_own)
+    part_own[...] = partial_own
+    wave_other = wave[pl.ds(first_other, half_rows)].astype(jnp.float32)
+    wave_own = wave[pl.ds(first_own, half_rows)].astype(jnp.float32)
+    norm = lanes(wave_own * wave_own)
+    correlation = lanes(part_out[...] * wave_other + part_own[...] * wave_own) + energy[0] * norm
+    stat_rows = lax.broadcasted_iota(jnp.int32, (8, 128), 0)
+    stats[rank] = jnp.where(stat_rows == 0, correlation, jnp.where(stat_rows == 1, norm, 0.0))
+
+    def stat_copy(peer, slot):
+        return pltpu.make_async_remote_copy(
+            src_ref=stats.at[slot],
+            dst_ref=stats.at[slot],
+            send_sem=stat_send.at[peer],
+            recv_sem=stat_recv.at[slot],
+            device_id={"blk": peer // 2, "sector": peer % 2},
+            device_id_type=pl.DeviceIdType.MESH,
+        )
+
+    for step in range(1, 2 * n):
+        stat_copy(lax.rem(rank + step, 2 * n), rank).start()
+
+    part_copy.wait_recv()
+    live = lax.broadcasted_iota(jnp.int32, (half_rows, cols), 0) + first_own < block_rows[0]
+    part_own[...] = jnp.where(
+        live, part_own[...] + part_in[...] + energy[0] * wave_own, 0.0
+    )
+    for step in range(1, 2 * n):
+        peer = lax.rem(rank + step, 2 * n)
+        stat_copy(peer, peer).wait_recv()
+    total = jnp.sum(stats[...], axis=0)
+    totals = jnp.sum(total, axis=1, keepdims=True)
+    quotient = totals[0:1] / totals[1:2]
+    rayleigh[0] = quotient[0, 0]
+    residual[...] = part_own[...] - quotient * wave_own
+
+    for block, piece, way, condition in sent:
+        under(condition, lambda: block_copy(block, piece, way).wait_send())
+    left_out.wait_send()
+    right_out.wait_send()
+    part_copy.wait_send()
+    for step in range(1, 2 * n):
+        stat_copy(lax.rem(rank + step, 2 * n), rank).wait_send()
+
+
+def line_shards(wavefunction, env_left, pattern, env_right, energy, block_rows):
+    n = lax.axis_size("blk")
+    rows, cols = wavefunction.shape
+    half_rows, half_cols = rows // 2, cols // 2
+    line_first, across_first = row_pieces(rows)
+    count = len(line_first) + len(across_first)
+    bf16, f32 = jnp.bfloat16, jnp.float32
+    dma = pltpu.SemaphoreType.DMA
+    smem = pl.BlockSpec(memory_space=pltpu.SMEM)
+    hbm = pl.BlockSpec(memory_space=pl.ANY)
+    residual, rayleigh = pl.pallas_call(
+        functools.partial(kernel, n),
+        out_shape=(
+            jax.ShapeDtypeStruct((half_rows, cols), f32),
+            jax.ShapeDtypeStruct((1,), f32),
+        ),
+        in_specs=[hbm, hbm, hbm, smem, smem, smem],
+        out_specs=(pl.BlockSpec(memory_space=pltpu.VMEM), smem),
+        scratch_shapes=[
+            pltpu.VMEM((rows, cols), bf16),
+            pltpu.VMEM((n, rows, half_cols), bf16),
+            pltpu.VMEM((n, 2 * rows, rows), bf16),
+            pltpu.VMEM((2, half_cols, cols), bf16),
+            pltpu.VMEM((2 * rows, half_cols), f32),
+            pltpu.VMEM((half_rows, cols), f32),
+            pltpu.VMEM((half_rows, cols), f32),
+            pltpu.VMEM((half_rows, cols), f32),
+            pltpu.VMEM((2 * n, 8, 128), f32),
+            dma((3,)),
+            dma((n, count, 3)),
+            dma((n, count)),
+            dma((3,)),
+            dma((3,)),
+            dma((2 * n,)),
+            dma((2 * n,)),
+        ],
+        compiler_params=pltpu.CompilerParams(
+            collective_id=0, has_side_effects=True, vmem_limit_bytes=40 * 1024 * 1024
+        ),
+        cost_estimate=pl.CostEstimate(
+            flops=6 * rows * rows * cols * n, bytes_accessed=4 * n * rows * rows, transcendentals=0
+        ),
+    )(wavefunction, env_left, env_right, pattern, energy, block_rows)
+    return residual, rayleigh
+
+
 def solution(mesh):
+    blk = mesh.shape["blk"]
+
+    def shards(wavefunction, env_left, pattern, env_right, energy, block_rows):
+        all_coupled = env_left.shape[1] == blk and blk % 2 == 0
+        body = line_shards if all_coupled else ring_shards
+        return body(wavefunction, env_left, pattern, env_right, energy, block_rows)
+
     return jax.shard_map(
         shards,
         mesh=mesh,

time: 193 us -> 43.4 us (0.22)
  waiting for transfers between devices: 83.1 us -> 0 us
  starting transfers between devices: 39.4 us -> 0 us
  blocking collectives: 34.5 us -> 0 us
  Pallas kernels: 0 us -> 34.4 us
  between operations: 18 us -> 3.67 us
  other arithmetic: 6.83 us -> 0 us
  matrix products: 5.26 us -> 0 us
    ppermute x8 -> x0, waiting for transfers between devices: 62.6 us -> none  [from_behind(): return lax.ppermute(value, axis, pairs)]
    ppermute x8 -> x0, starting transfers between devices: 39.4 us -> none  [from_behind(): return lax.ppermute(value, axis, pairs)]
    psum x1 -> x0, blocking collectives: 34.5 us -> none  [shards(): lax.psum((jnp.sum(own_wide * sigma_half), jnp.sum(own_wide * own_wide)),...]
    pallas_call x0 -> x1, Pallas kernels: none -> 34.4 us  [line_shards(): pl.pallas_call(functools.partial(kernel, n), out_shape=(jax.ShapeDtypeStr...]
    psum x1 -> x0, waiting for transfers between devices: 20.4 us -> none  [shards(): summed_terms = lax.psum(partial_sigma, 'sector')]
    dot_general x9 -> x0, matrix products: 5.26 us -> none  [the longest x8 3.24 us: add_term(): jnp.dot(term_env, pieces, preferred_element_type=jnp.float32)]
    while x7 -> x0, local copies, waits for them, and re-layouts: 5.16 us -> none
    unnamed x6 -> x8, local copies, waits for them, and re-layouts: 0.02 us -> 4.97 us
  transfers between devices with their start and end apart: 9 -> 0, of which waited for: 9 -> 0; matrix products, arithmetic and copies ran while one was open for 1% -> 0% of each run, Pallas kernels for 0% -> 0%
where the time goes in v1:
time: 43.4 us; the launch traced here: 43.1 us
  Pallas kernels  34.4 us (79%)
  local copies, waits for them, and re-layouts  4.97 us (11%)
  between operations  3.67 us (8%)
    pallas_call x1, Pallas kernels, line_shards(): pl.pallas_call(functools.partial(kernel, n), out_shape=(jax.ShapeDtypeStr...  34.4 us
    unnamed x8, local copies, waits for them, and re-layouts  4.97 us

profile of v1, /device:TPU:0, one launch (start us, length us, event | category | flops | bytes accessed | tf_op | source)
XLA Modules:
  0.0 43.1 jit_solution(3840751895889549365)
XLA Ops:
  1.9 0.7 %copy.8.pattern = s32[1,8,1]{2,1,0:T(8,128)S(1)} copy(s32[1,8,1]{1,2,0:T(1,128)} %param.8) | data formatting | bytes 64 | tf_op args[2]
  2.7 0.0 copy-start
  2.7 1.3 %copy-done = bf16[1,1,768,768]{3,2,1,0:T(8,128)(2,1)S(1)} copy-done((bf16[1,1,768,768]{3,2,1,0:T(8,128)(2,1)S(1)}, bf16[1,1,768,768]{3,2,1,0:T(8,128)(2,1)}, u32[]{:S(2)}) %copy-start) | copy-done | bytes 1179672
  3.9 0.0 copy-start.1
  3.9 1.2 %copy-done.1 = bf16[1,8,1,256,256]{4,3,2,1,0:T(8,128)(2,1)S(1)} copy-done((bf16[1,8,1,256,256]{4,3,2,1,0:T(8,128)(2,1)S(1)}, bf16[1,8,1,256,256]{4,3,2,1,0:T(8,128)(2,1)}, u32[]{:S(2)}) %copy-start.1) | copy-done | bytes 1048600
  5.1 0.0 copy-start.2
  5.2 1.0 %copy-done.2 = bf16[256,768]{1,0:T(8,128)(2,1)S(1)} copy-done((bf16[256,768]{1,0:T(8,128)(2,1)S(1)}, bf16[256,768]{1,0:T(8,128)(2,1)}, u32[]{:S(2)}) %copy-start.2) | copy-done | bytes 393240
  6.1 34.4 %shard_map.77 = (f32[128,768]{1,0:T(8,128)S(1)}, f32[1]{0:T(128)}) custom-call(bf16[256,768]{1,0:T(8,128)(2,1)S(1)} %copy-done.2, bf16[1,8,1,256,256]{4,3,2,1,0:T(8,128)(2,1)S(1)} %copy-done.1, bf16[1,1,768,768]{3,2,1,0:T(8,128)(2,1)S(1)} %copy-done, s32[1,8,1]{2,1,0:T(8,128)S(1)} %copy.8.pattern, f32[1]{0:T(128)S(6)} %copy.11.energy, s32[1]{0:T(128)S(6)} %copy.12.block_rows), custom_call_target="tpu_custom_call" | custom-call | flops 2415919104 | bytes 2097152 | tf_op jit(solution)/shard_map/pallas_call | solution.py:342
  40.6 0.7 %copy.13 = f32[128,768]{1,0:T(8,128)} copy(f32[128,768]{1,0:T(8,128)S(1)} %get-tuple-element.4) | data formatting | bytes 786432
Async XLA Ops:
  2.7 1.3 %copy-start = (bf16[1,1,768,768]{3,2,1,0:T(8,128)(2,1)S(1)}, bf16[1,1,768,768]{3,2,1,0:T(8,128)(2,1)}, u32[]{:S(2)}) copy-start(bf16[1,1,768,768]{3,2,1,0:T(8,128)(2,1)} %right_hbm.1) | copy-start | bytes 3538948
  3.9 1.2 %copy-start.1 = (bf16[1,8,1,256,256]{4,3,2,1,0:T(8,128)(2,1)S(1)}, bf16[1,8,1,256,256]{4,3,2,1,0:T(8,128)(2,1)}, u32[]{:S(2)}) copy-start(bf16[1,8,1,256,256]{4,3,2,1,0:T(8,128)(2,1)} %left_hbm.1) | copy-start | bytes 3145732
  5.1 1.0 %copy-start.2 = (bf16[256,768]{1,0:T(8,128)(2,1)S(1)}, bf16[256,768]{1,0:T(8,128)(2,1)}, u32[]{:S(2)}) copy-start(bf16[256,768]{1,0:T(8,128)(2,1)} %wave_hbm.1) | copy-start | bytes 1179652

commit v2 on v1

--- a/solution.py
+++ b/solution.py
@@ -60,13 +60,6 @@
     rayleigh = correlation / norm_sq
     residual = sigma_half - rayleigh * own_wide
     return (residual, rayleigh.reshape(1))
-
-
-def row_pieces(rows):
-    across = rows * 3 // 16 // 16 * 16
-    line = rows - across
-    front = (line // 2 + 15) // 16 * 16
-    return [(0, front), (front, line - front)], [(line, across)]
 
 
 def kernel(
@@ -106,9 +99,7 @@
     z, x = me // 2, me % 2
     beside = me + 1 - 2 * x
     rank = me * 2 + core
-    line_first, across_first = row_pieces(rows)
-    pieces = line_first + across_first
-    n_line = len(line_first)
+    at_end = jnp.logical_or(z == 0, z == lines - 1)
     has = {DOWN: z > 0, UP: z < lines - 1, ACROSS: None}
     toward = {DOWN: me - 2, UP: me + 2, ACROSS: beside}
 
@@ -124,14 +115,18 @@
     right_copy.start()
 
     barrier = pltpu.get_barrier_semaphore()
-    for step in range(1, 2 * n):
-        peer = lax.rem(rank + step, 2 * n)
+    def greet(block, which):
         pl.semaphore_signal(
             barrier,
             inc=1,
-            device_id={"blk": peer // 2, "sector": peer % 2},
+            device_id={"blk": block, "sector": which},
             device_id_type=pl.DeviceIdType.MESH,
         )
+
+    greet(me, other)
+    greet(beside, core)
+    for way in (DOWN, UP):
+        pl.when(has[way])(lambda: greet(toward[way], core))
 
     wave_copy.wait()
     row_ids = lax.broadcasted_iota(jnp.int32, (rows, cols), 0)
@@ -139,7 +134,7 @@
         wave.dtype
     )
     blocks[me] = wave[:, pl.ds(pl.multiple_of(core * half_cols, half_cols), half_cols)]
-    pl.semaphore_wait(barrier, 2 * n - 1)
+    pl.semaphore_wait(barrier, 2 + has[DOWN].astype(jnp.int32) + has[UP].astype(jnp.int32))
 
     sent = []
 
@@ -157,8 +152,7 @@
         return jnp.logical_and(first, second)
 
     def block_copy(block, piece, way):
-        start, size = pieces[piece]
-        part = blocks.at[block, pl.ds(start, size)]
+        part = blocks.at[block, pl.ds(piece * half_rows, half_rows)]
         return pltpu.make_async_remote_copy(
             src_ref=part,
             dst_ref=part,
@@ -176,12 +170,10 @@
     def receive(block, piece, condition=None):
         under(condition, lambda: block_copy(block, piece, ACROSS).wait_recv())
 
-    for piece in range(n_line):
-        for way in (DOWN, UP, ACROSS):
-            send(me, piece, way)
-    for piece in range(n_line, len(pieces)):
-        for way in (ACROSS, DOWN, UP):
-            send(me, piece, way)
+    for piece in range(2):
+        send(me, piece, DOWN)
+        send(me, piece, UP)
+        send(me, 1 - piece, ACROSS)
 
     def pair_copy(source, target, index):
         return pltpu.make_async_remote_copy(
@@ -197,7 +189,7 @@
     for slot in range(n):
         mine = left[slot, pl.ds(core * rows, rows)].astype(jnp.float32)
         left[slot, pl.ds(core * rows, rows)] = (
-            mine * pattern[0, slot, 0].astype(jnp.float32)
+            mine * pattern[slot].astype(jnp.float32)
         ).astype(left.dtype)
     own_left = left.at[:, pl.ds(core * rows, rows)]
     left_out = pair_copy(own_left, own_left, 0)
@@ -215,47 +207,73 @@
 
         under(condition, action)
 
+    def ends(distance):
+        return (
+            (beside + 2 * distance, z + distance == lines - 1, DOWN),
+            (beside - 2 * distance, z == distance, UP),
+        )
+
+    def sides(block, distance):
+        if distance == 0:
+            return ((block, None, None),)
+        return (
+            (block + 2 * distance, z + distance < lines, DOWN),
+            (block - 2 * distance, z >= distance, UP),
+        )
+
     def forward(distance):
-        sides = (
-            (me + 2 * distance, z + distance < lines, DOWN),
-            (me - 2 * distance, z >= distance, UP),
-        )
-        for piece in range(n_line):
-            for block, condition, way in sides:
+        for piece in range(2):
+            for block, condition, way in sides(me, distance):
                 receive(block, piece, condition)
                 send(block, piece, way, condition)
-                send(block, piece, ACROSS, condition)
-        for piece in range(n_line, len(pieces)):
-            if distance == 1:
-                receive(beside, piece)
-                send(beside, piece, DOWN)
-                send(beside, piece, UP)
-            for block, condition, way in sides:
-                for source in (block, block + 1 - 2 * x):
-                    receive(source, piece, condition)
-                    send(source, piece, way, condition)
-
-    def compute(distance):
-        if distance < lines:
-            accumulate(me + 2 * distance, z + distance < lines)
-            accumulate(me - 2 * distance, z >= distance)
-        near = distance - 1
-        sides = [(beside, None)]
-        if near:
-            sides = [(beside + 2 * near, z + near < lines), (beside - 2 * near, z >= near)]
-        for block, condition in sides:
-            for piece in range(n_line):
-                receive(block, piece, condition)
+                if piece == 0:
+                    send(block, piece, ACROSS, condition)
+            if piece == 1:
+                for block, condition, way in sides(me, distance):
+                    inner = both(condition, is_inner(distance, way))
+                    send(block, piece, ACROSS, inner)
+            if distance == 1 and piece == 0:
+                receive(beside, 1)
+                send(beside, 1, DOWN, at_end)
+                send(beside, 1, UP, at_end)
+
+    def is_inner(distance, way):
+        return z + distance < lines - 1 if way == DOWN else z > distance
+
+    def forward_ends(distance):
+        for block, condition, way in ends(distance):
+            receive(block, 1, condition)
+            send(block, 1, way, condition)
+
+    def own_line(distance):
+        for block, condition, _ in sides(me, distance):
             accumulate(block, condition)
 
-    forward(1)
-    left_out.wait_recv()
-    accumulate(me, fresh=True)
-    for distance in range(2, lines):
+    def other_line(distance):
+        for block, condition, way in sides(beside, distance):
+            receive(block, 0, condition)
+            if distance:
+                receive(block, 1, both(condition, is_inner(distance, way)))
+            accumulate(block, condition)
+
+    for distance in range(1, lines):
         forward(distance)
-        compute(distance - 1)
-    compute(lines - 1)
-    compute(lines)
+        if distance < lines - 1:
+            forward_ends(distance)
+        if distance == 1:
+            left_out.wait_recv()
+            accumulate(me, fresh=True)
+        else:
+            other_line(distance - 2)
+        own_line(distance)
+    if lines > 1:
+        other_line(lines - 2)
+        forward_ends(lines - 1)
+    else:
+        left_out.wait_recv()
+        accumulate(me, fresh=True)
+        receive(beside, 1)
+    other_line(lines - 1)
 
     right_copy.wait()
     right_out.wait_recv()
@@ -333,12 +351,10 @@
     n = lax.axis_size("blk")
     rows, cols = wavefunction.shape
     half_rows, half_cols = rows // 2, cols // 2
-    line_first, across_first = row_pieces(rows)
-    count = len(line_first) + len(across_first)
     bf16, f32 = jnp.bfloat16, jnp.float32
     dma = pltpu.SemaphoreType.DMA
     smem = pl.BlockSpec(memory_space=pltpu.SMEM)
-    hbm = pl.BlockSpec(memory_space=pl.ANY)
+    hbm = pl.BlockSpec(memory_space=pltpu.HBM)
     residual, rayleigh = pl.pallas_call(
         functools.partial(kernel, n),
         out_shape=(
@@ -358,20 +374,20 @@
             pltpu.VMEM((half_rows, cols), f32),
             pltpu.VMEM((2 * n, 8, 128), f32),
             dma((3,)),
-            dma((n, count, 3)),
-            dma((n, count)),
+            dma((n, 2, 3)),
+            dma((n, 2)),
             dma((3,)),
             dma((3,)),
             dma((2 * n,)),
             dma((2 * n,)),
         ],
         compiler_params=pltpu.CompilerParams(
-            collective_id=0, has_side_effects=True, vmem_limit_bytes=40 * 1024 * 1024
+            collective_id=0, has_side_effects=True, vmem_limit_bytes=60 * 1024 * 1024
         ),
         cost_estimate=pl.CostEstimate(
             flops=6 * rows * rows * cols * n, bytes_accessed=4 * n * rows * rows, transcendentals=0
         ),
-    )(wavefunction, env_left, env_right, pattern, energy, block_rows)
+    )(wavefunction, env_left, env_right, pattern.reshape(n), energy, block_rows)
     return residual, rayleigh
 
 

time: 43.4 us -> 36.4 us (0.84)
  Pallas kernels: 34.4 us -> 30.7 us
  local copies, waits for them, and re-layouts: 4.97 us -> 1.77 us
    pallas_call x1, Pallas kernels: 34.4 us -> 30.7 us  [line_shards(): pl.pallas_call(functools.partial(kernel, n), out_shape=(jax.ShapeDtypeStr...]
    unnamed x8 -> x1, local copies, waits for them, and re-layouts: 4.97 us -> 1.77 us
where the time goes in v2:
time: 36.4 us; the launch traced here: 36.2 us
  Pallas kernels  30.7 us (84%)
  between operations  3.68 us (10%)
  local copies, waits for them, and re-layouts  1.77 us (5%)
    pallas_call x1, Pallas kernels, line_shards(): pl.pallas_call(functools.partial(kernel, n), out_shape=(jax.ShapeDtypeStr...  30.7 us
    unnamed x1, local copies, waits for them, and re-layouts  1.77 us

profile of v2, /device:TPU:0, one launch (start us, length us, event | category | flops | bytes accessed | tf_op | source)
XLA Modules:
  0.0 36.2 jit_solution(3588451765364400963)
XLA Ops:
  1.9 30.7 %shard_map.77 = (f32[128,768]{1,0:T(8,128)}, f32[1]{0:T(128)}) custom-call(bf16[256,768]{1,0:T(8,128)(2,1)} %wave_hbm.1, bf16[1,8,1,256,256]{4,3,2,1,0:T(8,128)(2,1)} %left_hbm.1, bf16[1,1,768,768]{3,2,1,0:T(8,128)(2,1)} %right_hbm.1, s32[8]{0:T(128)} %bitcast.1, f32[1]{0:T(128)S(6)} %copy.10.energy, s32[1]{0:T(128)S(6)} %copy.11.block_rows), custom_call_target="tpu_custom_call" | custom-call | flops 2415919104 | bytes 2097152 | tf_op jit(solution)/shard_map/pallas_call | solution.py:358
  32.7 1.8 %copy.12 = f32[128,768]{1,0:T(8,128)} copy(f32[128,768]{1,0:T(8,128)} %get-tuple-element.4) | data formatting | bytes 786432

commit v3 on v2

--- a/solution.py
+++ b/solution.py
@@ -67,19 +67,21 @@
     wave_hbm,
     left_hbm,
     right_hbm,
+    pattern_hbm,
+    energy_hbm,
+    block_rows_hbm,
+    residual,
+    rayleigh,
     pattern,
     energy,
     block_rows,
-    residual,
-    rayleigh,
     wave,
     blocks,
     left,
     right,
     acc,
-    part_out,
+    partial,
     part_in,
-    part_own,
     stats,
     local_sem,
     send_sem,
@@ -110,9 +112,11 @@
     right_copy = pltpu.make_async_copy(
         right_hbm.at[0, 0, pl.ds(core * half_cols, half_cols)], right.at[core], local_sem.at[2]
     )
-    wave_copy.start()
-    left_copy.start()
-    right_copy.start()
+    scalars = [(block_rows_hbm, block_rows), (pattern_hbm, pattern), (energy_hbm, energy)]
+    scalar_copies = [
+        pltpu.make_async_copy(source, target, local_sem.at[3 + index])
+        for index, (source, target) in enumerate(scalars)
+    ]
 
     barrier = pltpu.get_barrier_semaphore()
     def greet(block, which):
@@ -128,7 +132,14 @@
     for way in (DOWN, UP):
         pl.when(has[way])(lambda: greet(toward[way], core))
 
+    wave_copy.start()
+    for copy in scalar_copies:
+        copy.start()
+    left_copy.start()
+    right_copy.start()
     wave_copy.wait()
+    for copy in scalar_copies:
+        copy.wait()
     row_ids = lax.broadcasted_iota(jnp.int32, (rows, cols), 0)
     wave[...] = jnp.where(row_ids < block_rows[0], wave[...].astype(jnp.float32), 0.0).astype(
         wave.dtype
@@ -278,17 +289,15 @@
     right_copy.wait()
     right_out.wait_recv()
 
-    def finish(first):
-        total = None
-        for term in range(2):
-            wide = acc[pl.ds(pl.multiple_of(term * rows + first, half_rows), half_rows)]
-            high = wide.astype(jnp.bfloat16)
-            low = (wide - high.astype(jnp.float32)).astype(jnp.bfloat16)
-            both_parts = jnp.concatenate([high, low], axis=0)
-            product = jnp.dot(both_parts, right[term], preferred_element_type=jnp.float32)
-            product = product[:half_rows] + product[half_rows:]
-            total = product if total is None else total + product
-        return total
+    wide = jnp.concatenate([acc[pl.ds(0, rows)], acc[pl.ds(rows, rows)]], axis=1)
+    high = wide.astype(jnp.bfloat16)
+    low = (wide - high.astype(jnp.float32)).astype(jnp.bfloat16)
+    product = jnp.dot(
+        jnp.concatenate([high, low], axis=0),
+        right[...].reshape(cols, cols),
+        preferred_element_type=jnp.float32,
+    )
+    partial[...] = product[:rows] + product[rows:]
 
     def lanes(values):
         summed = values[:, 0:128]
@@ -298,16 +307,11 @@
 
     first_other = pl.multiple_of(other * half_rows, half_rows)
     first_own = pl.multiple_of(core * half_rows, half_rows)
-    partial_other = finish(first_other)
-    part_out[...] = partial_other
-    part_copy = pair_copy(part_out, part_in, 2)
+    part_copy = pair_copy(partial.at[pl.ds(first_other, half_rows)], part_in, 2)
     part_copy.start()
-    partial_own = finish(first_own)
-    part_own[...] = partial_own
-    wave_other = wave[pl.ds(first_other, half_rows)].astype(jnp.float32)
     wave_own = wave[pl.ds(first_own, half_rows)].astype(jnp.float32)
     norm = lanes(wave_own * wave_own)
-    correlation = lanes(part_out[...] * wave_other + part_own[...] * wave_own) + energy[0] * norm
+    correlation = lanes(partial[...] * wave[...].astype(jnp.float32)) + energy[0] * norm
     stat_rows = lax.broadcasted_iota(jnp.int32, (8, 128), 0)
     stats[rank] = jnp.where(stat_rows == 0, correlation, jnp.where(stat_rows == 1, norm, 0.0))
 
@@ -321,30 +325,37 @@
             device_id_type=pl.DeviceIdType.MESH,
         )
 
-    for step in range(1, 2 * n):
-        stat_copy(lax.rem(rank + step, 2 * n), rank).start()
+    turn = 1 - 2 * (z < lines // 2).astype(jnp.int32)
+    peers = []
+    for step in range(lines):
+        line = lax.rem(lines - 1 - z + step * turn + lines * lines, lines)
+        peers += [line * 4 + place for place in range(4)]
+    for peer in peers:
+        pl.when(peer != rank)(lambda: stat_copy(peer, rank).start())
 
     part_copy.wait_recv()
     live = lax.broadcasted_iota(jnp.int32, (half_rows, cols), 0) + first_own < block_rows[0]
-    part_own[...] = jnp.where(
-        live, part_own[...] + part_in[...] + energy[0] * wave_own, 0.0
-    )
-    for step in range(1, 2 * n):
-        peer = lax.rem(rank + step, 2 * n)
-        stat_copy(peer, peer).wait_recv()
+    sigma = jnp.where(
+        live,
+        partial[pl.ds(first_own, half_rows)] + part_in[...] + energy[0] * wave_own,
+        0.0,
+    )
+    part_in[...] = sigma
+    for peer in range(2 * n):
+        pl.when(peer != rank)(lambda: stat_copy(peer, peer).wait_recv())
     total = jnp.sum(stats[...], axis=0)
     totals = jnp.sum(total, axis=1, keepdims=True)
     quotient = totals[0:1] / totals[1:2]
     rayleigh[0] = quotient[0, 0]
-    residual[...] = part_own[...] - quotient * wave_own
+    residual[...] = part_in[...] - quotient * wave_own
 
     for block, piece, way, condition in sent:
         under(condition, lambda: block_copy(block, piece, way).wait_send())
     left_out.wait_send()
     right_out.wait_send()
     part_copy.wait_send()
-    for step in range(1, 2 * n):
-        stat_copy(lax.rem(rank + step, 2 * n), rank).wait_send()
+    for peer in range(2 * n):
+        pl.when(peer != rank)(lambda: stat_copy(peer, rank).wait_send())
 
 
 def line_shards(wavefunction, env_left, pattern, env_right, energy, block_rows):
@@ -354,26 +365,28 @@
     bf16, f32 = jnp.bfloat16, jnp.float32
     dma = pltpu.SemaphoreType.DMA
     smem = pl.BlockSpec(memory_space=pltpu.SMEM)
-    hbm = pl.BlockSpec(memory_space=pltpu.HBM)
+    hbm = pl.BlockSpec(memory_space=pl.ANY)
     residual, rayleigh = pl.pallas_call(
         functools.partial(kernel, n),
         out_shape=(
             jax.ShapeDtypeStruct((half_rows, cols), f32),
             jax.ShapeDtypeStruct((1,), f32),
         ),
-        in_specs=[hbm, hbm, hbm, smem, smem, smem],
+        in_specs=[hbm] * 6,
         out_specs=(pl.BlockSpec(memory_space=pltpu.VMEM), smem),
         scratch_shapes=[
+            pltpu.SMEM((n,), jnp.int32),
+            pltpu.SMEM((1,), f32),
+            pltpu.SMEM((1,), jnp.int32),
             pltpu.VMEM((rows, cols), bf16),
             pltpu.VMEM((n, rows, half_cols), bf16),
             pltpu.VMEM((n, 2 * rows, rows), bf16),
             pltpu.VMEM((2, half_cols, cols), bf16),
             pltpu.VMEM((2 * rows, half_cols), f32),
-            pltpu.VMEM((half_rows, cols), f32),
-            pltpu.VMEM((half_rows, cols), f32),
+            pltpu.VMEM((rows, cols), f32),
             pltpu.VMEM((half_rows, cols), f32),
             pltpu.VMEM((2 * n, 8, 128), f32),
-            dma((3,)),
+            dma((6,)),
             dma((n, 2, 3)),
             dma((n, 2)),
             dma((3,)),
@@ -382,7 +395,7 @@
             dma((2 * n,)),
         ],
         compiler_params=pltpu.CompilerParams(
-            collective_id=0, has_side_effects=True, vmem_limit_bytes=60 * 1024 * 1024
+            collective_id=0, has_side_effects=True, vmem_limit_bytes=(53 * 1024 + 512) * 1024
         ),
         cost_estimate=pl.CostEstimate(
             flops=6 * rows * rows * cols * n, bytes_accessed=4 * n * rows * rows, transcendentals=0

time: 36.4 us -> 34.5 us (0.948)
  Pallas kernels: 30.7 us -> 29.2 us
  local copies, waits for them, and re-layouts: 1.77 us -> 1.4 us
    pallas_call x1, Pallas kernels: 30.7 us -> 29.2 us  [line_shards(): pl.pallas_call(functools.partial(kernel, n), out_shape=(jax.ShapeDtypeStr...]
    unnamed x1 -> x3, local copies, waits for them, and re-layouts: 1.77 us -> 1.4 us
where the time goes in v3:
time: 34.5 us; the launch traced here: 34.3 us
  Pallas kernels  29.2 us (85%)
  between operations  3.7 us (11%)
  local copies, waits for them, and re-layouts  1.4 us (4%)
    pallas_call x1, Pallas kernels, line_shards(): pl.pallas_call(functools.partial(kernel, n), out_shape=(jax.ShapeDtypeStr...  29.2 us
    unnamed x3, local copies, waits for them, and re-layouts  1.4 us

profile of v3, /device:TPU:0, one launch (start us, length us, event | category | flops | bytes accessed | tf_op | source)
XLA Modules:
  0.0 34.3 jit_solution(2541950964344617093)
XLA Ops:
  1.9 0.0 copy-start
  1.9 0.6 %copy-done = s32[1,8,1]{1,2,0:T(1,128)S(1)} copy-done((s32[1,8,1]{1,2,0:T(1,128)S(1)}, s32[1,8,1]{1,2,0:T(1,128)}, u32[]{:S(2)}) %copy-start) | copy-done | bytes 56
  2.6 29.2 %shard_map.77 = (f32[128,768]{1,0:T(8,128)S(1)}, f32[1]{0:T(128)}) custom-call(bf16[256,768]{1,0:T(8,128)(2,1)} %wave_hbm.1, bf16[1,8,1,256,256]{4,3,2,1,0:T(8,128)(2,1)} %left_hbm.1, bf16[1,1,768,768]{3,2,1,0:T(8,128)(2,1)} %right_hbm.1, s32[8]{0:T(128)S(1)} %bitcast.1, f32[1]{0:T(128)S(6)} %copy.10.energy_hbm, s32[1]{0:T(128)S(6)} %copy.11.block_rows_hbm), custom_call_target="tpu_custom_call" | custom-call | flops 2415919104 | bytes 2097152 | tf_op jit(solution)/shard_map/pallas_call | solution.py:369
  31.8 0.7 %copy.12 = f32[128,768]{1,0:T(8,128)} copy(f32[128,768]{1,0:T(8,128)S(1)} %get-tuple-element.4) | data formatting | bytes 786432
Async XLA Ops:
  1.9 0.7 %copy-start = (s32[1,8,1]{1,2,0:T(1,128)S(1)}, s32[1,8,1]{1,2,0:T(1,128)}, u32[]{:S(2)}) copy-start(s32[1,8,1]{1,2,0:T(1,128)} %param.8) | copy-start | bytes 100

commit v4 on v3

--- a/solution.py
+++ b/solution.py
@@ -8,6 +8,7 @@
 from jax.sharding import PartitionSpec as P
 
 DOWN, UP, ACROSS = 0, 1, 2
+CUTS = 2
 
 
 def from_behind(value, axis, steps):
@@ -94,6 +95,8 @@
     lines = n // 2
     rows, cols = wave.shape
     half_rows, half_cols = rows // 2, cols // 2
+    piece_rows = half_rows // CUTS
+    halves = (range(CUTS), range(CUTS, 2 * CUTS))
     middle = n // 2
     core = lax.axis_index("sector")
     me = lax.axis_index("blk")
@@ -163,7 +166,7 @@
         return jnp.logical_and(first, second)
 
     def block_copy(block, piece, way):
-        part = blocks.at[block, pl.ds(piece * half_rows, half_rows)]
+        part = blocks.at[block, pl.ds(piece * piece_rows, piece_rows)]
         return pltpu.make_async_remote_copy(
             src_ref=part,
             dst_ref=part,
@@ -181,10 +184,10 @@
     def receive(block, piece, condition=None):
         under(condition, lambda: block_copy(block, piece, ACROSS).wait_recv())
 
-    for piece in range(2):
+    for piece in range(2 * CUTS):
+        send(me, (piece + CUTS) % (2 * CUTS), ACROSS)
         send(me, piece, DOWN)
         send(me, piece, UP)
-        send(me, 1 - piece, ACROSS)
 
     def pair_copy(source, target, index):
         return pltpu.make_async_remote_copy(
@@ -233,28 +236,31 @@
         )
 
     def forward(distance):
-        for piece in range(2):
+        for piece in halves[0]:
             for block, condition, way in sides(me, distance):
                 receive(block, piece, condition)
                 send(block, piece, way, condition)
-                if piece == 0:
-                    send(block, piece, ACROSS, condition)
-            if piece == 1:
-                for block, condition, way in sides(me, distance):
-                    inner = both(condition, is_inner(distance, way))
-                    send(block, piece, ACROSS, inner)
-            if distance == 1 and piece == 0:
-                receive(beside, 1)
-                send(beside, 1, DOWN, at_end)
-                send(beside, 1, UP, at_end)
+                send(block, piece, ACROSS, condition)
+        if distance == 1:
+            for piece in halves[1]:
+                receive(beside, piece)
+                send(beside, piece, DOWN, at_end)
+                send(beside, piece, UP, at_end)
+        for piece in halves[1]:
+            for block, condition, way in sides(me, distance):
+                receive(block, piece, condition)
+                send(block, piece, way, condition)
+            for block, condition, way in sides(me, distance):
+                send(block, piece, ACROSS, both(condition, is_inner(distance, way)))
 
     def is_inner(distance, way):
         return z + distance < lines - 1 if way == DOWN else z > distance
 
     def forward_ends(distance):
-        for block, condition, way in ends(distance):
-            receive(block, 1, condition)
-            send(block, 1, way, condition)
+        for piece in halves[1]:
+            for block, condition, way in ends(distance):
+                receive(block, piece, condition)
+                send(block, piece, way, condition)
 
     def own_line(distance):
         for block, condition, _ in sides(me, distance):
@@ -262,9 +268,11 @@
 
     def other_line(distance):
         for block, condition, way in sides(beside, distance):
-            receive(block, 0, condition)
+            for piece in halves[0]:
+                receive(block, piece, condition)
             if distance:
-                receive(block, 1, both(condition, is_inner(distance, way)))
+                for piece in halves[1]:
+                    receive(block, piece, both(condition, is_inner(distance, way)))
             accumulate(block, condition)
 
     for distance in range(1, lines):
@@ -283,7 +291,8 @@
     else:
         left_out.wait_recv()
         accumulate(me, fresh=True)
-        receive(beside, 1)
+        for piece in halves[1]:
+            receive(beside, piece)
     other_line(lines - 1)
 
     right_copy.wait()
@@ -341,6 +350,13 @@
         0.0,
     )
     part_in[...] = sigma
+    for block, piece, way, condition in sent:
+        under(condition, lambda: block_copy(block, piece, way).wait_send())
+    left_out.wait_send()
+    right_out.wait_send()
+    part_copy.wait_send()
+    for peer in range(2 * n):
+        pl.when(peer != rank)(lambda: stat_copy(peer, rank).wait_send())
     for peer in range(2 * n):
         pl.when(peer != rank)(lambda: stat_copy(peer, peer).wait_recv())
     total = jnp.sum(stats[...], axis=0)
@@ -348,14 +364,6 @@
     quotient = totals[0:1] / totals[1:2]
     rayleigh[0] = quotient[0, 0]
     residual[...] = part_in[...] - quotient * wave_own
-
-    for block, piece, way, condition in sent:
-        under(condition, lambda: block_copy(block, piece, way).wait_send())
-    left_out.wait_send()
-    right_out.wait_send()
-    part_copy.wait_send()
-    for peer in range(2 * n):
-        pl.when(peer != rank)(lambda: stat_copy(peer, rank).wait_send())
 
 
 def line_shards(wavefunction, env_left, pattern, env_right, energy, block_rows):
@@ -387,8 +395,8 @@
             pltpu.VMEM((half_rows, cols), f32),
             pltpu.VMEM((2 * n, 8, 128), f32),
             dma((6,)),
-            dma((n, 2, 3)),
-            dma((n, 2)),
+            dma((n, 2 * CUTS, 3)),
+            dma((n, 2 * CUTS)),
             dma((3,)),
             dma((3,)),
             dma((2 * n,)),

time: 34.5 us -> 34 us (0.986)
  Pallas kernels: 29.2 us -> 28.7 us
    pallas_call x1, Pallas kernels: 29.2 us -> 28.7 us  [line_shards(): pl.pallas_call(functools.partial(kernel, n), out_shape=(jax.ShapeDtypeStr...]
where the time goes in v4:
time: 34 us; the launch traced here: 33.8 us
  Pallas kernels  28.7 us (84%)
  between operations  3.7 us (11%)
  local copies, waits for them, and re-layouts  1.4 us (4%)
    pallas_call x1, Pallas kernels, line_shards(): pl.pallas_call(functools.partial(kernel, n), out_shape=(jax.ShapeDtypeStr...  28.7 us
    unnamed x3, local copies, waits for them, and re-layouts  1.4 us

profile of v4, /device:TPU:0, one launch (start us, length us, event | category | flops | bytes accessed | tf_op | source)
XLA Modules:
  0.0 33.8 jit_solution(7043506253669157384)
XLA Ops:
  1.9 0.0 copy-start
  1.9 0.6 %copy-done = s32[1,8,1]{1,2,0:T(1,128)S(1)} copy-done((s32[1,8,1]{1,2,0:T(1,128)S(1)}, s32[1,8,1]{1,2,0:T(1,128)}, u32[]{:S(2)}) %copy-start) | copy-done | bytes 56
  2.6 28.7 %shard_map.77 = (f32[128,768]{1,0:T(8,128)S(1)}, f32[1]{0:T(128)}) custom-call(bf16[256,768]{1,0:T(8,128)(2,1)} %wave_hbm.1, bf16[1,8,1,256,256]{4,3,2,1,0:T(8,128)(2,1)} %left_hbm.1, bf16[1,1,768,768]{3,2,1,0:T(8,128)(2,1)} %right_hbm.1, s32[8]{0:T(128)S(1)} %bitcast.1, f32[1]{0:T(128)S(6)} %copy.10.energy_hbm, s32[1]{0:T(128)S(6)} %copy.11.block_rows_hbm), custom_call_target="tpu_custom_call" | custom-call | flops 2415919104 | bytes 2097152 | tf_op jit(solution)/shard_map/pallas_call | solution.py:377
  31.3 0.7 %copy.12 = f32[128,768]{1,0:T(8,128)} copy(f32[128,768]{1,0:T(8,128)S(1)} %get-tuple-element.4) | data formatting | bytes 786432
Async XLA Ops:
  1.9 0.7 %copy-start = (s32[1,8,1]{1,2,0:T(1,128)S(1)}, s32[1,8,1]{1,2,0:T(1,128)}, u32[]{:S(2)}) copy-start(s32[1,8,1]{1,2,0:T(1,128)} %param.8) | copy-start | bytes 100

commit v5 on v4

--- a/solution.py
+++ b/solution.py
@@ -83,6 +83,9 @@
     acc,
     partial,
     part_in,
+    weights,
+    tall_both,
+    bilinear,
     stats,
     local_sem,
     send_sem,
@@ -218,6 +221,9 @@
             slot = lax.rem(block - me + middle + n, n)
             product = jnp.dot(left[slot], blocks[block], preferred_element_type=jnp.float32)
             acc[...] = product if fresh else acc[...] + product
+            met = weights[slot] * blocks[block].astype(jnp.float32)
+            met = jnp.sum(met.reshape(rows // 8, 8, half_cols), axis=0)
+            bilinear[...] = met if fresh else bilinear[...] + met
 
         under(condition, action)
 
@@ -235,12 +241,13 @@
             (block - 2 * distance, z >= distance, UP),
         )
 
-    def forward(distance):
+    def forward(distance, between=lambda: None):
         for piece in halves[0]:
             for block, condition, way in sides(me, distance):
                 receive(block, piece, condition)
                 send(block, piece, way, condition)
                 send(block, piece, ACROSS, condition)
+            between()
         if distance == 1:
             for piece in halves[1]:
                 receive(beside, piece)
@@ -252,6 +259,7 @@
                 send(block, piece, way, condition)
             for block, condition, way in sides(me, distance):
                 send(block, piece, ACROSS, both(condition, is_inner(distance, way)))
+            between()
 
     def is_inner(distance, way):
         return z + distance < lines - 1 if way == DOWN else z > distance
@@ -275,52 +283,74 @@
                     receive(block, piece, both(condition, is_inner(distance, way)))
             accumulate(block, condition)
 
+    def weigh():
+        left_out.wait_recv()
+        right_copy.wait()
+        right_out.wait_recv()
+        sides_two = []
+        for term in range(2):
+            sides_two.append(
+                lax.dot_general(
+                    wave[...],
+                    right[term],
+                    (((1,), (1,)), ((), ())),
+                    preferred_element_type=jnp.float32,
+                )
+            )
+        tall = jnp.concatenate(sides_two, axis=0)
+        tall_high = tall.astype(jnp.bfloat16)
+        tall_low = (tall - tall_high.astype(jnp.float32)).astype(jnp.bfloat16)
+        tall_both[...] = jnp.concatenate([tall_high, tall_low], axis=1)
+
+    def weigh_slots(first, last):
+        def one(slot, carry):
+            product = lax.dot_general(
+                left[slot],
+                tall_both[...],
+                (((0,), (0,)), ((), ())),
+                preferred_element_type=jnp.float32,
+            )
+            weights[slot] = product[:, :half_cols] + product[:, half_cols:]
+            return carry
+
+        lax.fori_loop(first, last, one, 0)
+
+    todo = list(range(n))
+
+    def next_slots():
+        if todo:
+            weigh_slots(todo[0], todo[0] + 2)
+            del todo[:2]
+
     for distance in range(1, lines):
-        forward(distance)
+        forward(distance, next_slots if distance == 2 else lambda: None)
         if distance < lines - 1:
             forward_ends(distance)
         if distance == 1:
-            left_out.wait_recv()
-            accumulate(me, fresh=True)
+            weigh()
         else:
+            while todo:
+                next_slots()
+            if distance == 2:
+                accumulate(me, fresh=True)
+                own_line(1)
             other_line(distance - 2)
-        own_line(distance)
-    if lines > 1:
-        other_line(lines - 2)
-        forward_ends(lines - 1)
-    else:
-        left_out.wait_recv()
-        accumulate(me, fresh=True)
-        for piece in halves[1]:
-            receive(beside, piece)
+            own_line(distance)
+    other_line(lines - 2)
+    forward_ends(lines - 1)
     other_line(lines - 1)
-
-    right_copy.wait()
-    right_out.wait_recv()
-
-    wide = jnp.concatenate([acc[pl.ds(0, rows)], acc[pl.ds(rows, rows)]], axis=1)
-    high = wide.astype(jnp.bfloat16)
-    low = (wide - high.astype(jnp.float32)).astype(jnp.bfloat16)
-    product = jnp.dot(
-        jnp.concatenate([high, low], axis=0),
-        right[...].reshape(cols, cols),
-        preferred_element_type=jnp.float32,
-    )
-    partial[...] = product[:rows] + product[rows:]
 
     def lanes(values):
         summed = values[:, 0:128]
-        for column in range(128, cols, 128):
+        for column in range(128, values.shape[1], 128):
             summed = summed + values[:, column : column + 128]
         return jnp.sum(summed, axis=0, keepdims=True)
 
     first_other = pl.multiple_of(other * half_rows, half_rows)
     first_own = pl.multiple_of(core * half_rows, half_rows)
-    part_copy = pair_copy(partial.at[pl.ds(first_other, half_rows)], part_in, 2)
-    part_copy.start()
     wave_own = wave[pl.ds(first_own, half_rows)].astype(jnp.float32)
     norm = lanes(wave_own * wave_own)
-    correlation = lanes(partial[...] * wave[...].astype(jnp.float32)) + energy[0] * norm
+    correlation = lanes(bilinear[...]) + energy[0] * norm
     stat_rows = lax.broadcasted_iota(jnp.int32, (8, 128), 0)
     stats[rank] = jnp.where(stat_rows == 0, correlation, jnp.where(stat_rows == 1, norm, 0.0))
 
@@ -342,6 +372,18 @@
     for peer in peers:
         pl.when(peer != rank)(lambda: stat_copy(peer, rank).start())
 
+    wide = jnp.concatenate([acc[pl.ds(0, rows)], acc[pl.ds(rows, rows)]], axis=1)
+    high = wide.astype(jnp.bfloat16)
+    low = (wide - high.astype(jnp.float32)).astype(jnp.bfloat16)
+    product = jnp.dot(
+        jnp.concatenate([high, low], axis=0),
+        right[...].reshape(cols, cols),
+        preferred_element_type=jnp.float32,
+    )
+    partial[...] = product[:rows] + product[rows:]
+
+    part_copy = pair_copy(partial.at[pl.ds(first_other, half_rows)], part_in, 2)
+    part_copy.start()
     part_copy.wait_recv()
     live = lax.broadcasted_iota(jnp.int32, (half_rows, cols), 0) + first_own < block_rows[0]
     sigma = jnp.where(
@@ -393,6 +435,9 @@
             pltpu.VMEM((2 * rows, half_cols), f32),
             pltpu.VMEM((rows, cols), f32),
             pltpu.VMEM((half_rows, cols), f32),
+            pltpu.VMEM((n, rows, half_cols), f32),
+            pltpu.VMEM((2 * rows, cols), bf16),
+            pltpu.VMEM((8, half_cols), f32),
             pltpu.VMEM((2 * n, 8, 128), f32),
             dma((6,)),
             dma((n, 2 * CUTS, 3)),
@@ -416,7 +461,7 @@
     blk = mesh.shape["blk"]
 
     def shards(wavefunction, env_left, pattern, env_right, energy, block_rows):
-        all_coupled = env_left.shape[1] == blk and blk % 2 == 0
+        all_coupled = env_left.shape[1] == blk and blk % 2 == 0 and blk >= 6
         body = line_shards if all_coupled else ring_shards
         return body(wavefunction, env_left, pattern, env_right, energy, block_rows)
 

time: 34 us -> 33.4 us (0.982)
  Pallas kernels: 28.7 us -> 28.2 us
    pallas_call x1, Pallas kernels: 28.7 us -> 28.2 us  [line_shards(): pl.pallas_call(functools.partial(kernel, n), out_shape=(jax.ShapeDtypeStr...]
where the time goes in v5:
time: 33.4 us; the launch traced here: 33.3 us
  Pallas kernels  28.2 us (84%)
  between operations  3.7 us (11%)
  local copies, waits for them, and re-layouts  1.4 us (4%)
    pallas_call x1, Pallas kernels, line_shards(): pl.pallas_call(functools.partial(kernel, n), out_shape=(jax.ShapeDtypeStr...  28.2 us
    unnamed x3, local copies, waits for them, and re-layouts  1.4 us

profile of v5, /device:TPU:0, one launch (start us, length us, event | category | flops | bytes accessed | tf_op | source)
XLA Modules:
  0.0 33.3 jit_solution(8224103832416949033)
XLA Ops:
  1.9 0.0 copy-start
  1.9 0.6 %copy-done = s32[1,8,1]{1,2,0:T(1,128)S(1)} copy-done((s32[1,8,1]{1,2,0:T(1,128)S(1)}, s32[1,8,1]{1,2,0:T(1,128)}, u32[]{:S(2)}) %copy-start) | copy-done | bytes 56
  2.6 28.2 %shard_map.77 = (f32[128,768]{1,0:T(8,128)S(1)}, f32[1]{0:T(128)}) custom-call(bf16[256,768]{1,0:T(8,128)(2,1)} %wave_hbm.1, bf16[1,8,1,256,256]{4,3,2,1,0:T(8,128)(2,1)} %left_hbm.1, bf16[1,1,768,768]{3,2,1,0:T(8,128)(2,1)} %right_hbm.1, s32[8]{0:T(128)S(1)} %bitcast.1, f32[1]{0:T(128)S(6)} %copy.10.energy_hbm, s32[1]{0:T(128)S(6)} %copy.11.block_rows_hbm), custom_call_target="tpu_custom_call" | custom-call | flops 2415919104 | bytes 2097152 | tf_op jit(solution)/shard_map/pallas_call | solution.py:419
  30.7 0.7 %copy.12 = f32[128,768]{1,0:T(8,128)} copy(f32[128,768]{1,0:T(8,128)S(1)} %get-tuple-element.4) | data formatting | bytes 786432
Async XLA Ops:
  1.9 0.7 %copy-start = (s32[1,8,1]{1,2,0:T(1,128)S(1)}, s32[1,8,1]{1,2,0:T(1,128)}, u32[]{:S(2)}) copy-start(s32[1,8,1]{1,2,0:T(1,128)} %param.8) | copy-start | bytes 100
